TPU v7x, 32 devices: a whole 2x2x4 slice. The times are simulated.
32 devices in a mesh: gx: 4 (over y, x), gy: 8 (over z, core).
Axes of the slice: x: 2, y: 2, z: 4, core: 2. Of those that a mesh axis runs over, the one named last changes fastest.
Arguments:
- tokens: bfloat16 [512, 2048], P('gy', 'gx'), may hold values from -6 to 6
- gain: bfloat16 [2048], P('gx'), may hold values from 0.5 to 1.5
- w_router: bfloat16 [2048, 8], P('gx'), may hold values from -0.25 to 0.25
- expert_query_weight: bfloat16 [8, 2048, 16, 128], P(None, 'gx', 'gy'), may hold values from -0.25 to 0.25
- key_value_weight: bfloat16 [2048, 16, 256], P('gx', 'gy'), may hold values from -0.125 to 0.125
- expert_output_weight: bfloat16 [8, 16, 128, 2048], P(None, 'gy', None, 'gx'), may hold values from -0.25 to 0.25
- cache_keys: bfloat16 [4, 16, 4096, 128], P('gx', 'gy'), may hold values from -1220 to 1220
- cached_value_slots: bfloat16 [4, 16, 4096, 128], P('gx', 'gy'), may hold values from -6 to 6
- lengths: int32 [4], replicated, may hold values from 1 to 4096, 10240 in all
- deal: int32 [4], replicated, may hold values from 0 to 3, each once
- route: int32 [512, 2], replicated, may hold values from 0 to 7, all different within a row
Outputs:
- mixed: bfloat16 [512, 2048], P('gy', 'gx')
Inputs may be any that keep to these rules, and one draw needn't show every extreme that they name: `lengths`: each request's cache holds between 1 and 4096 keys, and the longest holds exactly 4096. deal[r] is the cache slot of request r; every slot is used once. `route`: each token names 2 different attention experts.
All inputs are finite; a program needn't handle non-finite values.
Results may differ from a plain program's by a relative error of at most 0.01.
The roundings to bfloat16 on the way count: a program that leaves them out, or rounds other values in their place, can miss the bound.
Values may be sent and summed in bfloat16 or wider, within the bound.
A program may use at most 64 MiB of HBM per device.

v0:
```python
import jax
import jax.numpy as jnp
from jax import lax
from jax.sharding import PartitionSpec as P

masked_score = -1e30
norm_eps = 1e-06


def expert_onehot(route_rows, experts):
    return (route_rows[:, :, None] == jnp.arange(experts, dtype=jnp.int32)[None, None, :]).astype(
        jnp.float32
    )


def absorb(carry_state, scores, value_rows):
    running_max, running_sum, accumulated = carry_state
    new_max = jnp.maximum(running_max, jnp.max(scores, axis=2))
    shrink = jnp.exp(running_max - new_max)
    weights = jnp.exp(scores - new_max[:, :, None])
    running_sum = running_sum * shrink + jnp.sum(weights, axis=2)
    accumulated = accumulated * shrink[:, :, None] + jnp.einsum(
        "hrk,hkd->hrd", weights.astype(jnp.bfloat16), value_rows, preferred_element_type=jnp.float32
    )
    return (new_max, running_sum, accumulated)


def per_device(
    tokens,
    gain,
    w_router,
    expert_query_weight,
    key_value_weight,
    expert_output_weight,
    cache_keys,
    cached_value_slots,
    lengths,
    deal,
    route,
):
    requests = lengths.shape[0]
    experts = expert_query_weight.shape[0]
    heads_local = expert_query_weight.shape[2]
    head_dim = expert_query_weight.shape[3]
    top_count = route.shape[1]
    gathered = lax.all_gather(tokens, "gy", axis=0, tiled=True)
    total_rows, local_width = gathered.shape
    new_len = total_rows // requests
    full_width = local_width * lax.axis_size("gx")
    slot_index = lax.axis_index("gx")
    inverse = jnp.zeros((requests,), jnp.int32).at[deal].set(jnp.arange(requests, dtype=jnp.int32))
    ordered = jnp.take(gathered.reshape(requests, new_len, local_width), inverse, axis=0).reshape(
        total_rows, local_width
    )
    slot_route = jnp.take(route.reshape(requests, new_len, top_count), inverse, axis=0).reshape(
        total_rows, top_count
    )
    widened = ordered.astype(jnp.float32)
    squares = jnp.sum(widened * widened, axis=1)
    scaled_input = (widened * gain.astype(jnp.float32)[None, :]).astype(jnp.bfloat16)
    router_part = jnp.dot(scaled_input, w_router, preferred_element_type=jnp.float32)
    query_part = jnp.einsum(
        "td,edhk->tehk", scaled_input, expert_query_weight, preferred_element_type=jnp.float32
    )
    keyval_part = jnp.einsum(
        "td,dhk->thk", scaled_input, key_value_weight, preferred_element_type=jnp.float32
    )
    my_route = lax.dynamic_slice_in_dim(slot_route, slot_index * new_len, new_len, 0)
    my_onehot = expert_onehot(my_route, experts)
    query_all, keyval_sums, router_sums, square_sums = (
        lax.psum_scatter(query_part, "gx", scatter_dimension=0, tiled=True),
        lax.psum_scatter(keyval_part, "gx", scatter_dimension=0, tiled=True),
        lax.psum_scatter(router_part, "gx", scatter_dimension=0, tiled=True),
        lax.psum_scatter(squares, "gx", scatter_dimension=0, tiled=True),
    )
    query_totals = jnp.sum(my_onehot[:, :, :, None, None] * query_all[:, None], axis=2)
    inverse_root_mean = lax.rsqrt(square_sums / full_width + norm_eps)
    logits = router_sums * inverse_root_mean[:, None]
    chosen = jnp.sum(my_onehot * logits[:, None, :], axis=2)
    gate_gap = chosen[:, 0] - chosen[:, 1]
    gate_weights = jnp.stack([jax.nn.sigmoid(gate_gap), jax.nn.sigmoid(-gate_gap)], axis=1).astype(
        jnp.bfloat16
    )
    query_matrix = (query_totals * inverse_root_mean[:, None, None, None]).astype(jnp.bfloat16)
    key_value_rows = (keyval_sums * inverse_root_mean[:, None, None]).astype(jnp.bfloat16)
    query_rows = new_len * top_count
    query_by_head = jnp.transpose(query_matrix, (2, 0, 1, 3)).reshape(
        heads_local, query_rows, head_dim
    )
    fresh_keyval = jnp.transpose(key_value_rows, (1, 0, 2))
    fresh_keys = fresh_keyval[:, :, :head_dim]
    fresh_values = fresh_keyval[:, :, head_dim:]
    length = jnp.take(lengths, jnp.take(inverse, slot_index))
    local_keys = cache_keys[0]
    local_values = cached_value_slots[0]
    cache_span = local_keys.shape[1]
    key_block = min(1024, cache_span)
    score_scale = head_dim ** (-0.5)
    initial = (
        jnp.full((heads_local, query_rows), masked_score, jnp.float32),
        jnp.zeros((heads_local, query_rows), jnp.float32),
        jnp.zeros((heads_local, query_rows, head_dim), jnp.float32),
    )

    def visit_block(block_index, carry_state):
        first_key = block_index * key_block
        key_rows = lax.dynamic_slice_in_dim(local_keys, first_key, key_block, 1)
        value_rows = lax.dynamic_slice_in_dim(local_values, first_key, key_block, 1)
        scores = (
            jnp.einsum("hrd,hkd->hrk", query_by_head, key_rows, preferred_element_type=jnp.float32)
            * score_scale
        )
        visible = first_key + jnp.arange(key_block, dtype=jnp.int32) < length
        scores = jnp.where(visible[None, None, :], scores, masked_score)
        return absorb(carry_state, scores, value_rows)

    block_count = (length + key_block - 1) // key_block
    carry_state = lax.fori_loop(0, block_count, visit_block, initial)
    fresh_scores = (
        jnp.einsum("hrd,hkd->hrk", query_by_head, fresh_keys, preferred_element_type=jnp.float32)
        * score_scale
    )
    causal = (
        jnp.arange(new_len, dtype=jnp.int32)[None, :]
        <= (jnp.arange(query_rows, dtype=jnp.int32) // top_count)[:, None]
    )
    fresh_scores = jnp.where(causal[None], fresh_scores, masked_score)
    running_max, running_sum, accumulated = absorb(carry_state, fresh_scores, fresh_values)
    attended_output = (accumulated / running_sum[:, :, None]).astype(jnp.bfloat16)
    attended_output = jnp.transpose(
        attended_output.reshape(heads_local, new_len, top_count, head_dim), (1, 2, 0, 3)
    ).reshape(new_len, top_count * heads_local * head_dim)
    all_attended, all_gates = (
        lax.all_gather(attended_output, "gx", axis=0, tiled=True),
        lax.all_gather(gate_weights, "gx", axis=0, tiled=True),
    )
    token_attended = jnp.take(
        all_attended.reshape(requests, new_len, top_count * heads_local * head_dim), deal, axis=0
    ).reshape(total_rows, top_count, heads_local, head_dim)
    token_gates = (
        jnp.take(all_gates.reshape(requests, new_len, top_count), deal, axis=0)
        .reshape(total_rows, top_count)
        .astype(jnp.float32)
    )
    wide_output = expert_output_weight.astype(jnp.float32)
    piece = token_attended.astype(jnp.float32)
    mixing = expert_onehot(route, experts) * token_gates[:, :, None]
    folded = jnp.einsum("tse,tshd->tehd", mixing, piece, precision=lax.Precision.HIGHEST)
    output_sum = lax.psum_scatter(
        jnp.einsum("tehd,ehdo->to", folded, wide_output, precision=lax.Precision.HIGHEST),
        "gy",
        scatter_dimension=0,
        tiled=True,
    )
    return output_sum.astype(jnp.bfloat16)


def solution(mesh):
    placed = (
        P("gy", "gx"),
        P("gx"),
        P("gx", None),
        P(None, "gx", "gy", None),
        P("gx", "gy", None),
        P(None, "gy", None, "gx"),
        P("gx", "gy", None, None),
        P("gx", "gy", None, None),
        P(),
        P(),
        P(),
    )
    return jax.shard_map(
        per_device, mesh=mesh, in_specs=placed, out_specs=P("gy", "gx"), check_vma=False
    )
```

profile of v0, /device:TPU:0, one launch (start us, length us, event | category | flops | bytes accessed | tf_op | source)
XLA Modules:
  0.0 219.1 jit_solution(2774754171072262589)
XLA Ops:
  6.5 0.8 compare_select_fusion.2
  7.3 0.6 scatter_custom_fusion
  8.0 0.7 convert_element_type.57
  8.7 16.8 %all_gather.9 = bf16[512,512]{1,0:T(8,128)(2,1)S(1)} all-gather(bf16[64,512]{1,0:T(8,128)(2,1)} %param.15), channel_id=1, replica_groups=mesh['gx'=4,'gy'=8] {'gy'}, dimensions={0}, use_global_device_ids=true | all-gather | bytes 589824 | tf_op jit(solution)/shard_map/all_gather | solution.py:46
  25.4 0.6 gather_fusion.2
  26.0 0.1 select_convert_fusion
  26.2 0.1 fusion.25
  26.3 0.9 fusion.54
  27.2 0.0 reduce-scatter.9.cloned.1.call-start
  27.2 2.5 %fusion.30 = f32[512,2,256]{2,0,1:T(8,128)} fusion(bf16[512,512]{1,0:T(8,128)(2,1)S(1)} %fusion.25, bf16[512,2,256]{2,1,0:T(2,128)(2,1)} %param.19), kind=kOutput, calls=%fused_computation.44 | convolution fusion | flops 268435456 | bytes 2097152 | tf_op jit(solution)/shard_map/td,dhk->thk/dot_general | solution.py:65
  29.7 0.0 reduce-scatter.9.cloned.1.call-update
  29.8 0.0 reduce-scatter.7.cloned.1.call-start
  29.8 3.2 %fusion.17 = f32[512,8,2,128]{3,0,2,1:T(8,128)} fusion(bf16[8,512,2,128]{3,2,1,0:T(2,128)(2,1)S(1)} %copy-done, bf16[512,512]{1,0:T(8,128)(2,1)S(1)} %fusion.25), kind=kOutput, calls=%fused_computation.28 | convolution fusion | flops 1073741824 | bytes 6815744 | tf_op jit(solution)/shard_map/td,edhk->tehk/dot_general | solution.py:62
  33.0 0.0 reduce-scatter.7.cloned.1.call-update
  33.0 0.0 reduce-scatter.11.cloned.1.call-start
  33.1 0.6 dynamic-slice.4
  34.3 0.6 dynamic-slice.5
  35.6 0.1 copy.79
  35.7 0.6 gather_fusion
  36.3 0.1 broadcast_bitcast_fusion
  36.4 0.1 dynamic-slice.8
  36.5 0.1 copy.81
  36.7 0.6 dynamic-slice.6
  37.8 0.3 multiply_reduce_fusion.1
  38.1 9.9 %all-reduce = f32[512]{0:T(512)S(1)} all-reduce(f32[512]{0:T(512)S(1)} %bitcast.82), channel_id=3, replica_groups=mesh['gx'=4,'gy'=8] {'gx'}, use_global_device_ids=true, to_apply=%region_3.5.clone | all-reduce | flops 512 | bytes 4096
  48.0 0.1 fusion.48
  48.1 0.1 broadcast_bitcast_fusion.1
  48.2 2.5 %reduce-scatter.5.cloned.1.call-done = f32[128,8]{0,1:T(8,128)} async-done(((f32[512,8]{0,1:T(8,128)}), f32[128,8]{0,1:T(8,128)}) %reduce-scatter.5.cloned.1.call-update) | async-done | bytes 4112 | tf_op jit(solution)/shard_map/reduce_scatter | solution.py:73
  50.7 0.7 broadcast_multiply_fusion
  51.5 7.9 %all_gather.10 = bf16[512,2]{0,1:T(2,128)(2,1)S(1)} all-gather(bf16[128,2]{0,1:T(2,128)(2,1)S(1)} %pad_maximum_fusion), channel_id=1, replica_groups=mesh['gx'=4,'gy'=8] {'gx'}, dimensions={0}, use_global_device_ids=true | all-gather | bytes 2560 | tf_op jit(solution)/shard_map/all_gather | solution.py:135
  59.3 0.6 gather_fusion.1
  59.9 0.9 copy.80
  60.8 20.6 %reduce-scatter.9.cloned.1.call-done = f32[128,2,256]{2,0,1:T(8,128)} async-done(((f32[512,2,256]{2,0,1:T(8,128)}), f32[128,2,256]{2,0,1:T(8,128)}) %reduce-scatter.9.cloned.1.call-update) | async-done | bytes 262160 | tf_op jit(solution)/shard_map/reduce_scatter | solution.py:72
  81.4 1.0 fusion.41
  82.4 54.9 %reduce-scatter.7.cloned.1.call-done = f32[128,8,2,128]{3,0,2,1:T(8,128)} async-done(((f32[512,8,2,128]{3,0,2,1:T(8,128)}), f32[128,8,2,128]{3,0,2,1:T(8,128)}) %reduce-scatter.7.cloned.1.call-update) | async-done | bytes 1048592 | tf_op jit(solution)/shard_map/reduce_scatter | solution.py:71
  137.4 1.8 copy.83
  139.2 0.9 multiply_reduce_fusion
  140.1 0.2 multiply_convert_fusion.1
  140.4 16.4 %while.16 = (s32[]{:T(128)}, f32[2,256]{1,0:T(2,128)S(1)}, f32[2,256]{1,0:T(2,128)S(1)}, f32[2,256,128]{2,1,0:T(8,128)S(1)}, s32[]{:T(128)}, /*index=5*/s32[]{:T...) while((s32[]{:T(128)}, f32[2,256]{1,0:T(2,128)S(1)}, ...), condition=%wide.region_10.12_spmd, body=%wide.region_7.0_spmd.sunk | while | flops 274336768 | bytes 8032443 | solution.py:118
  140.4 1.5 bitcast_reduce_fusion.2
  141.9 0.5 fusion.66
  142.5 2.0 convolution_add_fusion.3
  144.5 1.5 bitcast_reduce_fusion.2
  146.0 0.5 fusion.66
  146.5 2.0 convolution_add_fusion.3
  148.6 1.5 bitcast_reduce_fusion.2
  150.1 0.5 fusion.66
  150.6 2.0 convolution_add_fusion.3
  152.7 1.5 bitcast_reduce_fusion.2
  154.2 0.5 fusion.66
  154.7 2.0 convolution_add_fusion.3
  156.7 0.2 fusion.53
  157.0 0.1 fusion.38
  157.1 0.3 fusion.24
  157.3 0.1 copy.88
  157.5 10.1 %all_gather.11 = bf16[512,512]{0,1:T(8,128)(2,1)S(1)} all-gather(bf16[128,512]{0,1:T(8,128)(2,1)S(1)} %bitcast.78), channel_id=1, replica_groups=mesh['gx'=4,'gy'=8] {'gx'}, dimensions={0}, use_global_device_ids=true | all-gather | bytes 655360 | tf_op jit(solution)/shard_map/all_gather | solution.py:134
  167.6 0.2 copy.89
  167.8 0.6 gather_fusion.3
  168.4 0.1 broadcast_select_fusion
  168.5 0.1 reshape.135
  168.6 4.6 %fusion.27 = f32[512,8,2,128]{3,1,2,0:T(8,128)S(1)} fusion(bf16[512,2,2,128]{3,2,1,0:T(2,128)(2,1)S(1)} %reshape.135, f32[512,2]{1,0:T(8,128)} %copy.80, s32[512,2]{1,0:T(8,128)S(1)} %copy.79), kind=kOutput, calls=%fused_computation.42 | convolution fusion | flops 25182208 | bytes 4726784 | tf_op jit(solution)/shard_map/tse,tshd->tehd/dot_general | solution.py:148
  173.2 5.2 %fusion.19 = f32[512,512]{1,0:T(8,128)} fusion(bf16[8,2,128,512]{3,2,1,0:T(8,128)(2,1)S(1)} %copy-done.3, f32[512,8,2,128]{3,1,2,0:T(8,128)S(1)} %fusion.27), kind=kOutput, calls=%fused_computation.31 | convolution fusion | flops 6442450944 | bytes 7340032 | tf_op jit(solution)/shard_map/tehd,ehdo->to/dot_general | solution.py:150
  178.5 32.5 %reduce-scatter.11.cloned.1.call-done = f32[64,512]{1,0:T(8,128)} async-done(((f32[512,512]{1,0:T(8,128)}), f32[64,512]{1,0:T(8,128)}) %reduce-scatter.11.cloned.1.call-update) | async-done | bytes 131088 | tf_op jit(solution)/shard_map/reduce_scatter | solution.py:149
  211.0 1.5 convert_element_type.67
  (53 shorter events, 0.4 us)
Async XLA Ops:
  6.5 23.3 %copy-start = (bf16[8,512,2,128]{3,2,1,0:T(2,128)(2,1)S(1)}, bf16[8,512,2,128]{3,2,1,0:T(2,128)(2,1)}, u32[]{:S(2)}) copy-start(bf16[8,512,2,128]{3,2,1,0:T(2,128)(2,1)} %param.18) | copy-start | bytes 6291460
  6.5 44.2 %reduce-scatter.5.cloned.1.call-start = ((), (), s32[]{:S(2)}) async-start(), calls=%async_computation.4 | async-start | bytes 20480 | tf_op jit(solution)/shard_map/reduce_scatter | solution.py:73
  25.4 0.9 copy-start.2
  27.2 54.2 %reduce-scatter.9.cloned.1.call-start = ((), (), s32[]{:S(2)}) async-start(), calls=%async_computation.6 | async-start | bytes 1310720 | tf_op jit(solution)/shard_map/reduce_scatter | solution.py:72
  29.8 107.6 %reduce-scatter.7.cloned.1.call-start = ((), (), s32[]{:S(2)}) async-start(), calls=%async_computation.5 | async-start | bytes 5242880 | tf_op jit(solution)/shard_map/reduce_scatter | solution.py:71
  33.0 1.3 copy-start.4
  33.0 2.6 %copy-start.1 = (s32[512,2]{0,1:T(2,128)S(1)}, s32[512,2]{0,1:T(2,128)}, u32[]{:S(2)}) copy-start(s32[512,2]{0,1:T(2,128)} %param.25) | copy-start | bytes 12292
  33.0 3.6 %copy-start.6 = (u32[32]{0:T(128)S(1)}, u32[32]{0:T(128)}, u32[]{:S(2)}) copy-start(u32[32]{0:T(128)} %constant.187) | copy-start | bytes 388
  33.0 15.1 %copy-start.5 = (s32[4]{0:T(128)S(1)}, s32[4]{0:T(128)}, u32[]{:S(2)}) copy-start(s32[4]{0:T(128)} %param.24) | copy-start | bytes 52
  33.0 178.0 %reduce-scatter.11.cloned.1.call-start = ((), (), s32[]{:S(2)}) async-start(), calls=%async_computation.7 | async-start | bytes 1179648 | tf_op jit(solution)/shard_map/reduce_scatter | solution.py:149
  168.6 4.6 %copy-start.3 = (bf16[8,2,128,512]{3,2,1,0:T(8,128)(2,1)S(1)}, bf16[8,2,128,512]{3,2,1,0:T(8,128)(2,1)}, u32[]{:S(2)}) copy-start(bf16[8,2,128,512]{3,2,1,0:T(8,128)(2,1)} %param.20) | copy-start | bytes 6291460
Sparse Core Ops, SparseCore 0:
  27.3 23.3 reduce-scatter.4
  53.6 27.7 reduce-scatter.8
  84.6 52.6 reduce-scatter.6
  178.6 32.3 reduce-scatter.10
where the time goes:
time: 220 us; the launch traced here: 219 us
  waiting for transfers between devices  111 us (50%)
  blocking collectives  44.7 us (20%)
  matrix products  30.8 us (14%)
  between operations  15.2 us (7%)
  other arithmetic  8.93 us (4%)
  local copies, waits for them, and re-layouts  8.48 us (4%)
    reduce_scatter x1, waiting for transfers between devices, per_device(): lax.psum_scatter(query_part, 'gx', scatter_dimension=0, tiled=True)  54.9 us
    reduce_scatter x1, waiting for transfers between devices, per_device(): lax.psum_scatter(jnp.einsum('tehd,ehdo->to', folded, wide_output, precisi...  32.5 us
    reduce_scatter x1, waiting for transfers between devices, per_device(): lax.psum_scatter(keyval_part, 'gx', scatter_dimension=0, tiled=True)  20.6 us
    all_gather x1, blocking collectives, per_device(): gathered = lax.all_gather(tokens, 'gy', axis=0, tiled=True)  16.8 us
    all_gather x1, blocking collectives, per_device(): lax.all_gather(attended_output, 'gx', axis=0, tiled=True)  10.1 us
    unnamed x1, blocking collectives  9.92 us
    dot_general x5, matrix products, absorb(): jnp.einsum('hrk,hkd->hrd', weights.astype(jnp.bfloat16), value_rows, pref...  8.22 us
    all_gather x1, blocking collectives, per_device(): lax.all_gather(gate_weights, 'gx', axis=0, tiled=True)  7.87 us
  transfers between devices with their start and end apart: 4, of which 4 were waited for; matrix products, arithmetic and copies ran while one was open for 6% of the time, Pallas kernels for 0%

commit v1 on v0

v1 whole, which is shorter than its diff:
```python
import functools
import math

import jax
import jax.numpy as jnp
from jax import lax
from jax.experimental import pallas as pl
from jax.experimental.pallas import tpu as pltpu
from jax.sharding import PartitionSpec as P

MESH = pl.DeviceIdType.MESH
masked_score = -1e30
norm_eps = 1e-06


def kernel(
    nx, ny, full_width,
    tokens_ref, gain_ref, wr_ref, route_ref, lengths_ref, deal_ref,
    wq_hbm, wkv_hbm, wo_hbm, k_hbm, v_hbm,
    out_ref,
    xg, wq, wkv, wo, kc, vc,
    qsend, qrecv, gsend, grecv, kvsend, kvrecv, tile, gall,
    qmat, scores, maxes, fkey, fval, agbuf, outs, psend, precv, zsend, zrecv,
    ld_sem, a_send, a_recv, f_send, q_send, q_recv, g_send, g_recv, kv_send, kv_recv,
    t_send, t_recv, at_send, at_recv, p_send, p_recv, z_send, z_recv,
):
    f32, bf16 = jnp.float32, jnp.bfloat16
    mx, my = lax.axis_index("gx"), lax.axis_index("gy")
    nz = ny // 2
    mz, core = my // 2, lax.rem(my, 2)
    partner = my + 1 - 2 * core
    tb = tokens_ref.shape[0]
    experts = wq.shape[0]
    heads, cache, hd = kc.shape
    new = xg.shape[0] // nx
    rows = 2 * new
    per_req = new // tb

    def remote(src, dst, ss, rs, dev):
        return pltpu.make_async_remote_copy(
            src_ref=src, dst_ref=dst, send_sem=ss, recv_sem=rs, device_id=dev, device_id_type=MESH
        )

    def atx(c):
        return (c, my)

    def aty(c):
        return (mx, c)

    loads = [
        pltpu.make_async_copy(s, d, ld_sem.at[i])
        for i, (s, d) in enumerate(
            ((wq_hbm, wq), (wkv_hbm, wkv), (k_hbm, kc), (v_hbm, vc), (wo_hbm, wo))
        )
    ]
    for load in loads:
        load.start()

    barrier = pltpu.get_barrier_semaphore()
    for d in range(1, nx):
        pl.semaphore_signal(barrier, inc=1, device_id=atx(lax.rem(mx + d, nx)), device_id_type=MESH)
    pl.semaphore_signal(barrier, inc=1, device_id=aty(partner), device_id_type=MESH)
    for d in range(1, nz):
        pl.semaphore_signal(
            barrier, inc=1, device_id=aty(lax.rem(mz + d, nz) * 2 + core), device_id_type=MESH
        )
    pl.semaphore_wait(barrier, nx - 1 + nz)

    def block(b):
        return xg.at[pl.ds(pl.multiple_of(b * tb, tb), tb)]

    def a_copy(d):
        return remote(tokens_ref, block(my), a_send.at[d], a_recv.at[my],
                      aty(lax.rem(mz + d, nz) * 2 + core))

    def a_in(b, ss):
        return remote(block(b), block(b), ss, a_recv.at[b], aty(partner))

    for d in range(1, nz):
        a_copy(d).start()
    own = remote(tokens_ref, block(my), a_send.at[0], a_recv.at[my], aty(partner))
    own.start()
    block(my)[...] = tokens_ref[...]
    for d in range(1, nz):
        b = lax.rem(mz + nz - d, nz) * 2 + core
        c = a_in(b, f_send.at[d])
        c.wait_recv()
        c.start()
    a_in(partner, f_send.at[0]).wait_recv()
    for d in range(1, nz):
        b = lax.rem(mz + nz - d, nz) * 2 + 1 - core
        a_in(b, f_send.at[d]).wait_recv()

    def pick(keys, wanted, values, shape):
        acc = values(0)
        for i in range(1, nx):
            acc = jnp.where(jnp.full(shape, keys(i) - wanted) == 0, values(i), acc)
        return acc

    def deal_of(i):
        return deal_ref[i]

    def route_of(c):
        return pick(deal_of, c, lambda i: route_ref[i * new:(i + 1) * new, :], (1, route_ref.shape[1]))

    tile[...] = jnp.zeros_like(tile)
    gain = gain_ref[...].astype(f32)
    loads[0].wait()

    def scaled_of(c):
        x = pick(deal_of, c, lambda i: xg[i * new:(i + 1) * new, :].astype(f32), (1, xg.shape[1]))
        return x, (x * gain).astype(bf16)

    def q_copy(c, d):
        return remote(qsend.at[d], qrecv.at[mx], q_send.at[d], q_recv.at[mx], atx(c))

    def g_copy(c, d):
        return remote(gsend.at[d], grecv.at[mx], g_send.at[d], g_recv.at[mx], atx(c))

    def kv_copy(c, d):
        return remote(kvsend.at[d], kvrecv.at[mx], kv_send.at[d], kv_recv.at[mx], atx(c))

    def project(c):
        x, xs = scaled_of(c)
        route = route_of(c)
        r0, r1 = route[:, 0:1], route[:, 1:2]
        q0 = jnp.zeros((new, heads * hd), f32)
        q1 = q0
        for e in range(experts):
            y = jnp.dot(xs, wq[e], preferred_element_type=f32)
            q0 = jnp.where(r0 == e, y, q0)
            q1 = jnp.where(r1 == e, y, q1)
        tile[:, 0:experts] = jnp.dot(xs, wr_ref[...], preferred_element_type=f32)
        tile[:, experts:experts + 1] = jnp.sum(x * x, axis=1, keepdims=True)
        return q0, q1, tile[...].T[0:16]

    def send_q(d, carry):
        c = lax.rem(mx + d, nx)
        q0, q1, g = project(c)
        qsend[d, 0:new] = q0
        qsend[d, new:rows] = q1
        gsend[d] = g
        g_copy(c, d).start()
        q_copy(c, d).start()
        return carry

    lax.fori_loop(1, nx, send_q, 0)
    q0, q1, g = project(mx)
    qsend[0, 0:new] = q0
    qsend[0, new:rows] = q1
    gsend[0] = g
    loads[1].wait()

    def send_kv(d, carry):
        c = lax.rem(mx + d, nx)
        kvsend[d] = jnp.dot(scaled_of(c)[1], wkv[...], preferred_element_type=f32)
        kv_copy(c, d).start()
        return carry

    lax.fori_loop(1, nx, send_kv, 0)
    kvsend[0] = jnp.dot(scaled_of(mx)[1], wkv[...], preferred_element_type=f32)

    for d in range(1, nx):
        c = lax.rem(mx + d, nx)
        remote(gsend.at[d], grecv.at[c], g_send.at[d], g_recv.at[c], atx(c)).wait_recv()
    g = gsend[0]
    for d in range(1, nx):
        g = g + grecv[lax.rem(mx + d, nx)]
    tile[...] = jnp.zeros_like(tile)
    tile[0:16] = g
    cols = tile[...].T
    inv = lax.rsqrt(cols[:, experts:experts + 1] * (1.0 / full_width) + norm_eps)
    inv2 = jnp.concatenate([inv, inv], axis=0)
    route = route_of(mx)
    lane = lax.broadcasted_iota(jnp.int32, (new, 128), 1)
    logits = cols * inv
    c0 = jnp.sum(jnp.where(lane == route[:, 0:1], logits, 0.0), axis=1, keepdims=True)
    c1 = jnp.sum(jnp.where(lane == route[:, 1:2], logits, 0.0), axis=1, keepdims=True)
    g0 = jax.nn.sigmoid(c0 - c1).astype(bf16).astype(f32)
    g1 = jax.nn.sigmoid(c1 - c0).astype(bf16).astype(f32)
    gall[mx] = jnp.where(lane == 0, g0, jnp.where(lane == 1, g1, 0.0)).T[0:8]

    def t_copy(d, at):
        c = lax.rem(mx + d, nx)
        return remote(gall.at[at], gall.at[at], t_send.at[d], t_recv.at[at], atx(c))

    for d in range(1, nx):
        t_copy(d, mx).start()

    for d in range(1, nx):
        c = lax.rem(mx + d, nx)
        remote(qsend.at[d], qrecv.at[c], q_send.at[d], q_recv.at[c], atx(c)).wait_recv()
    q = qsend[0]
    for d in range(1, nx):
        q = q + qrecv[lax.rem(mx + d, nx)]
    qmat[...] = (q * inv2).astype(bf16)

    bk = min(512, cache)
    length = pick(deal_of, mx, lambda i: jnp.full((1, bk), lengths_ref[i]), (1, bk))
    loads[2].wait()
    nt = (((1,), (1,)), ((), ()))
    maxes[...] = jnp.full(maxes.shape, masked_score, f32)

    def fold_max(h, s):
        m = maxes[h]
        for j in range(s.shape[1] // 128):
            m = jnp.maximum(m, s[:, j * 128:(j + 1) * 128])
        maxes[h] = m

    def score_block(i, carry):
        first = pl.multiple_of(i * bk, bk)
        visible = first + lax.broadcasted_iota(jnp.int32, (1, bk), 1) < length
        for h in range(heads):
            s = lax.dot_general(qmat[:, h * hd:(h + 1) * hd], kc[h, pl.ds(first, bk), :], nt,
                                preferred_element_type=f32)
            s = jnp.where(visible, s, masked_score)
            scores[h, :, pl.ds(first, bk)] = s
            fold_max(h, s)
        return carry

    lax.fori_loop(0, cache // bk, score_block, 0)

    for d in range(1, nx):
        c = lax.rem(mx + d, nx)
        remote(kvsend.at[d], kvrecv.at[c], kv_send.at[d], kv_recv.at[c], atx(c)).wait_recv()
    kv = kvsend[0]
    for d in range(1, nx):
        kv = kv + kvrecv[lax.rem(mx + d, nx)]
    kv = (kv * inv).astype(bf16)
    row = lax.rem(lax.broadcasted_iota(jnp.int32, (rows, new), 0), new)
    causal = lax.broadcasted_iota(jnp.int32, (rows, new), 1) <= row
    loads[3].wait()
    unit = hd ** -0.5 * math.log2(math.e)

    def at_copy(h, d, at):
        c = lax.rem(mx + d, nx)
        return remote(agbuf.at[at, h], agbuf.at[at, h], at_send.at[h, d], at_recv.at[h, at], atx(c))

    for h in range(heads):
        fkey[...] = kv[:, h * 2 * hd:h * 2 * hd + hd]
        fval[...] = kv[:, h * 2 * hd + hd:(h + 1) * 2 * hd]
        s = lax.dot_general(qmat[:, h * hd:(h + 1) * hd], fkey[...], nt, preferred_element_type=f32)
        s = jnp.where(causal, s, masked_score)
        fold_max(h, s)
        m = jnp.max(maxes[h], axis=1, keepdims=True)
        w = jnp.exp2((s - m) * unit)
        total = w
        acc = jnp.dot(w.astype(bf16), fval[...], preferred_element_type=f32)

        def weigh(i, carry, h=h, m=m):
            total, acc = carry
            first = pl.multiple_of(i * bk, bk)
            w = jnp.exp2((scores[h, :, pl.ds(first, bk)] - m) * unit)
            for j in range(bk // 128):
                total = total + w[:, j * 128:(j + 1) * 128]
            acc = acc + jnp.dot(w.astype(bf16), vc[h, pl.ds(first, bk), :], preferred_element_type=f32)
            return total, acc

        total, acc = lax.fori_loop(0, cache // bk, weigh, (total, acc))
        agbuf[mx, h] = (acc / jnp.sum(total, axis=1, keepdims=True)).astype(bf16)
        for d in range(1, nx):
            at_copy(h, d, mx).start()

    loads[4].wait()
    tile[...] = jnp.zeros_like(tile)

    def produce(c):
        route = route_of(c)
        rr = jnp.concatenate([route[:, 0:1], route[:, 1:2]], axis=0)
        tile[0:8] = gall[c]
        gate = tile[...].T
        a = [agbuf[c, h] for h in range(heads)]
        a = jnp.concatenate(a, axis=1) if heads > 1 else a[0]
        y = jnp.zeros((rows, wo.shape[2]), f32)
        for e in range(experts):
            y = y + jnp.dot(jnp.where(rr == e, a, jnp.zeros_like(a)), wo[e],
                            preferred_element_type=f32)
        outs[c] = gate[:, 0:1] * y[0:new] + gate[:, 1:2] * y[new:rows]

    produce(mx)

    def arrive(d, carry):
        c = lax.rem(mx + nx - d, nx)
        t_copy(d, c).wait_recv()
        for h in range(heads):
            at_copy(h, d, c).wait_recv()
        produce(c)
        return carry

    lax.fori_loop(1, nx, arrive, 0)

    def partial(b):
        slot = deal_ref[b // per_req]
        part = pl.ds(pl.multiple_of(lax.rem(b, per_req) * tb, tb), tb)
        return pick(lambda i: i, slot, lambda i: outs[i, part, :], (1, outs.shape[2]))

    for z in range(nz):
        psend[z] = partial(z * 2 + 1 - core)
    pc = remote(psend, precv, p_send, p_recv, aty(partner))
    pc.start()
    pc.wait_recv()

    def z_copy(d, at):
        return remote(zsend.at[d], zrecv.at[at], z_send.at[d], z_recv.at[at],
                      aty(lax.rem(mz + d, nz) * 2 + core))

    for d in range(nz - 1, 0, -1):
        z = lax.rem(mz + d, nz)
        zsend[d] = (partial(z * 2 + core) + precv[z]).astype(bf16)
        z_copy(d, mz).start()
    total = partial(my) + precv[mz]
    for d in range(1, nz):
        z = lax.rem(mz + nz - d, nz)
        z_copy(d, z).wait_recv()
        total = total + zrecv[z].astype(f32)
    out_ref[...] = total.astype(bf16)

    own.wait_send()
    for d in range(1, nz):
        a_copy(d).wait_send()
        a_in(lax.rem(mz + nz - d, nz) * 2 + core, f_send.at[d]).wait_send()
        z_copy(d, mz).wait_send()
    pc.wait_send()
    for d in range(1, nx):
        c = lax.rem(mx + d, nx)
        g_copy(c, d).wait_send()
        q_copy(c, d).wait_send()
        kv_copy(c, d).wait_send()
        t_copy(d, mx).wait_send()
        for h in range(heads):
            at_copy(h, d, mx).wait_send()


def per_device(nx, ny, tokens, gain, w_router, wq, wkv, wo, ck, cv, lengths, deal, route):
    f32, bf16 = jnp.float32, jnp.bfloat16
    tb, width = tokens.shape
    experts, _, heads, hd = wq.shape
    out_w = wo.shape[3]
    cache = ck.shape[2]
    nz = ny // 2
    total = tb * ny
    new = total // nx
    rows = 2 * new
    hw = heads * hd
    dma = pltpu.SemaphoreType.DMA
    vm = pltpu.VMEM
    vspec = pl.BlockSpec(memory_space=pltpu.VMEM)
    sspec = pl.BlockSpec(memory_space=pltpu.SMEM)
    aspec = pl.BlockSpec(memory_space=pl.ANY)
    return pl.pallas_call(
        functools.partial(kernel, nx, ny, width * nx),
        out_shape=jax.ShapeDtypeStruct((tb, out_w), bf16),
        in_specs=[vspec] * 4 + [sspec] * 2 + [aspec] * 5,
        out_specs=vspec,
        scratch_shapes=[
            vm((total, width), bf16),
            vm((experts, width, hw), bf16),
            vm((width, 2 * hw), bf16),
            vm((experts, hw, out_w), bf16),
            vm((heads, cache, hd), bf16),
            vm((heads, cache, hd), bf16),
            vm((nx, rows, hw), f32),
            vm((nx, rows, hw), f32),
            vm((nx, 16, new), f32),
            vm((nx, 16, new), f32),
            vm((nx, new, 2 * hw), f32),
            vm((nx, new, 2 * hw), f32),
            vm((new, 128), f32),
            vm((nx, 8, new), f32),
            vm((rows, hw), bf16),
            vm((heads, rows, cache), f32),
            vm((heads, rows, 128), f32),
            vm((new, hd), bf16),
            vm((new, hd), bf16),
            vm((nx, heads, rows, hd), bf16),
            vm((nx, new, out_w), f32),
            vm((nz, tb, out_w), f32),
            vm((nz, tb, out_w), f32),
            vm((nz, tb, out_w), bf16),
            vm((nz, tb, out_w), bf16),
            dma((5,)), dma((nz,)), dma((ny,)), dma((nz,)),
            dma((nx,)), dma((nx,)), dma((nx,)), dma((nx,)), dma((nx,)), dma((nx,)),
            dma((nx,)), dma((nx,)), dma((heads, nx)), dma((heads, nx)),
            dma, dma, dma((nz,)), dma((nz,)),
        ],
        compiler_params=pltpu.CompilerParams(
            collective_id=0, has_side_effects=True, vmem_limit_bytes=48 * 1024 * 1024
        ),
    )(
        tokens, gain.reshape(1, width), w_router, route, lengths, deal,
        wq.reshape(experts, width, hw), wkv.reshape(width, 2 * hw),
        wo.reshape(experts, hw, out_w), ck[0], cv[0],
    )


def solution(mesh):
    placed = (
        P("gy", "gx"), P("gx"), P("gx", None), P(None, "gx", "gy", None), P("gx", "gy", None),
        P(None, "gy", None, "gx"), P("gx", "gy", None, None), P("gx", "gy", None, None),
        P(), P(), P(),
    )
    return jax.shard_map(
        functools.partial(per_device, mesh.shape["gx"], mesh.shape["gy"]),
        mesh=mesh, in_specs=placed, out_specs=P("gy", "gx"), check_vma=False,
    )
```

time: 220 us -> 70.9 us (0.32)
  waiting for transfers between devices: 111 us -> 0 us
  Pallas kernels: 0 us -> 61.5 us
  blocking collectives: 44.7 us -> 0 us
  matrix products: 30.8 us -> 0 us
  between operations: 15.2 us -> 0.09 us
  other arithmetic: 8.93 us -> 0 us
    reduce_scatter x4 -> x0, waiting for transfers between devices: 111 us -> none  [the longest x1 54.9 us: per_device(): lax.psum_scatter(query_part, 'gx', scatter_dimension=0, tiled=True)]
    pallas_call x0 -> x1, Pallas kernels: none -> 61.5 us  [per_device(): pl.pallas_call(functools.partial(kernel, nx, ny, width * nx), out_shape=j...]
    all_gather x3 -> x0, blocking collectives: 34.7 us -> none  [the longest x1 16.8 us: per_device(): gathered = lax.all_gather(tokens, 'gy', axis=0, tiled=True)]
    dot_general x15 -> x0, matrix products: 30.8 us -> none  [the longest x5 8.22 us: absorb(): jnp.einsum('hrk,hkd->hrd', weights.astype(jnp.bfloat16), value_rows, pref...]
    unnamed x1 -> x0, blocking collectives: 9.92 us -> none
    unnamed x16 -> x12, local copies, waits for them, and re-layouts: 0.76 us -> 5.05 us
    reshape x2, local copies, waits for them, and re-layouts: 0.25 us -> 3.86 us  [the longest x1 3.18 us: per_device(): wq.reshape(experts, width, hw)]
    reduce_sum x8 -> x0, other arithmetic: 3.27 us -> none  [the longest x5 2.1 us: absorb(): running_sum = running_sum * shrink + jnp.sum(weights, axis=2)]
  transfers between devices with their start and end apart: 4 -> 0, of which waited for: 4 -> 0; matrix products, arithmetic and copies ran while one was open for 6% -> 0% of each run, Pallas kernels for 0% -> 0%
where the time goes in v1:
time: 70.9 us; the launch traced here: 70.5 us
  Pallas kernels  61.5 us (87%)
  local copies, waits for them, and re-layouts  8.91 us (13%)
    pallas_call x1, Pallas kernels, per_device(): pl.pallas_call(functools.partial(kernel, nx, ny, width * nx), out_shape=j...  61.5 us
    unnamed x12, local copies, waits for them, and re-layouts  5.05 us
    reshape x1, local copies, waits for them, and re-layouts, per_device(): wq.reshape(experts, width, hw)  3.18 us

profile of v1, /device:TPU:0, one launch (start us, length us, event | category | flops | bytes accessed | tf_op | source)
XLA Modules:
  0.0 70.5 jit_solution(5087376950983569293)
XLA Ops:
  0.0 0.7 reshape.12.gain_ref
  0.7 0.9 %copy.12.wr_ref = bf16[512,8]{1,0:T(8,128)(2,1)S(1)} copy(bf16[512,8]{0,1:T(8,128)(2,1)} %param.13) | data formatting | bytes 16384 | tf_op args[2]
  1.5 0.8 %copy.13.route_ref = s32[512,2]{1,0:T(8,128)S(1)} copy(s32[512,2]{0,1:T(2,128)} %param.21) | data formatting | bytes 8192 | tf_op args[10]
  2.4 1.1 %copy.14 = bf16[64,8,2,256]{3,1,2,0:T(8,128)(2,1)S(1)} copy(bf16[64,8,2,256]{3,2,1,0:T(2,128)(2,1)} %bitcast.9) | data formatting | bytes 1048576
  3.5 0.0 copy-start.1
  3.5 0.0 copy-start.2
  3.5 0.0 copy-start.3
  3.6 3.2 %reshape.13.wq_hbm = bf16[8,512,256]{2,1,0:T(8,128)(2,1)S(1)} reshape(bf16[8,512,2,128]{3,2,1,0:T(2,128)(2,1)} %param.14) | data formatting | bytes 4194304 | tf_op jit(solution)/shard_map/reshape | solution.py:391
  6.7 0.0 copy-done.1
  6.7 0.0 copy-done.2
  6.8 0.0 copy-done.3
  6.8 0.0 copy-start
  6.8 1.6 %copy-done = bf16[8,2,128,512]{3,2,1,0:T(8,128)(2,1)S(1)} copy-done((bf16[8,2,128,512]{3,2,1,0:T(8,128)(2,1)S(1)}, bf16[8,2,128,512]{3,2,1,0:T(8,128)(2,1)}, u32[]{:S(2)}) %copy-start) | copy-done | bytes 2097176
  8.4 61.5 %shard_map.109 = bf16[64,512]{1,0:T(8,128)(2,1)S(1)} custom-call(bf16[64,512]{1,0:T(8,128)(2,1)S(1)} %copy-done.1, bf16[1,512]{1,0:T(2,128)(2,1)S(1)} %reshape.12.gain_ref, bf16[512,8]{1,0:T(8,128)(2,1)S(1)} %copy.12.wr_ref, s32[512,2]{1,0:T(8,128)S(1)} %copy.13.route_ref, s32[4]{0:T(128)S(1)} %copy-done.2, s32[4]{0:T(128)S(1)} %copy-done.3, ...), custom_call_target="tpu_custom_call" | custom-call | tf_op jit(solution)/shard_map/pallas_call | solution.py:350
  69.9 0.6 copy.16
Async XLA Ops:
  3.5 3.2 %copy-start.1 = (bf16[64,512]{1,0:T(8,128)(2,1)S(1)}, bf16[64,512]{1,0:T(8,128)(2,1)}, u32[]{:S(2)}) copy-start(bf16[64,512]{1,0:T(8,128)(2,1)} %tokens_ref.1) | copy-start | bytes 196612
  3.5 3.2 %copy-start.2 = (s32[4]{0:T(128)S(1)}, s32[4]{0:T(128)}, u32[]{:S(2)}) copy-start(s32[4]{0:T(128)} %lengths_ref.1) | copy-start | bytes 52
  3.5 3.2 %copy-start.3 = (s32[4]{0:T(128)S(1)}, s32[4]{0:T(128)}, u32[]{:S(2)}) copy-start(s32[4]{0:T(128)} %deal_ref.1) | copy-start | bytes 52
  6.8 1.6 %copy-start = (bf16[8,2,128,512]{3,2,1,0:T(8,128)(2,1)S(1)}, bf16[8,2,128,512]{3,2,1,0:T(8,128)(2,1)}, u32[]{:S(2)}) copy-start(bf16[8,2,128,512]{3,2,1,0:T(8,128)(2,1)} %param.16) | copy-start | bytes 6291460

commit v2 on v1

--- a/solution.py
+++ b/solution.py
@@ -18,13 +18,14 @@
     tokens_ref, gain_ref, wr_ref, route_ref, lengths_ref, deal_ref,
     wq_hbm, wkv_hbm, wo_hbm, k_hbm, v_hbm,
     out_ref,
-    xg, wq, wkv, wo, kc, vc,
-    qsend, qrecv, gsend, grecv, kvsend, kvrecv, tile, gall,
+    xg, wq4, wkv3, wq, wkv, wo, kc, vc, rcol,
+    qsend, qrecv, gsend, grecv, kvsend, kvrecv, kvown, tile, gall,
     qmat, scores, maxes, fkey, fval, agbuf, outs, psend, precv, zsend, zrecv,
     ld_sem, a_send, a_recv, f_send, q_send, q_recv, g_send, g_recv, kv_send, kv_recv,
     t_send, t_recv, at_send, at_recv, p_send, p_recv, z_send, z_recv,
 ):
     f32, bf16 = jnp.float32, jnp.bfloat16
+    nt = (((1,), (1,)), ((), ()))
     mx, my = lax.axis_index("gx"), lax.axis_index("gy")
     nz = ny // 2
     mz, core = my // 2, lax.rem(my, 2)
@@ -50,7 +51,7 @@
     loads = [
         pltpu.make_async_copy(s, d, ld_sem.at[i])
         for i, (s, d) in enumerate(
-            ((wq_hbm, wq), (wkv_hbm, wkv), (k_hbm, kc), (v_hbm, vc), (wo_hbm, wo))
+            ((wq_hbm, wq4), (wkv_hbm, wkv3), (k_hbm, kc), (v_hbm, vc), (wo_hbm, wo))
         )
     ]
     for load in loads:
@@ -81,6 +82,43 @@
     own = remote(tokens_ref, block(my), a_send.at[0], a_recv.at[my], aty(partner))
     own.start()
     block(my)[...] = tokens_ref[...]
+    def pick(keys, wanted, values, shape):
+        acc = values(0)
+        for i in range(1, nx):
+            acc = jnp.where(jnp.full(shape, keys(i) - wanted) == 0, values(i), acc)
+        return acc
+
+    def deal_of(i):
+        return deal_ref[i]
+
+    def route_of(c):
+        return rcol[c]
+
+    tile[...] = jnp.zeros_like(tile)
+    gain = gain_ref[...].astype(f32).reshape(1, gain_ref.shape[0])
+
+    def route_column(c, carry):
+        slots = route_ref.shape[0]
+        tile[0:slots] = pick(
+            deal_of, c, lambda i: route_ref[:, i * new:(i + 1) * new].astype(f32), (slots, new)
+        )
+        rcol[c] = tile[...].T
+        return carry
+
+    lax.fori_loop(0, nx, route_column, 0)
+    loads[0].wait()
+
+    def relayout(e, carry):
+        for h in range(heads):
+            wq[e, :, h * hd:(h + 1) * hd] = wq4[e, :, h, :]
+        return carry
+
+    lax.fori_loop(0, experts, relayout, 0)
+    loads[1].wait()
+    for h in range(heads):
+        wkv[:, h * 2 * hd:(h + 1) * 2 * hd] = wkv3[:, h, :]
+
+
     for d in range(1, nz):
         b = lax.rem(mz + nz - d, nz) * 2 + core
         c = a_in(b, f_send.at[d])
@@ -90,22 +128,6 @@
     for d in range(1, nz):
         b = lax.rem(mz + nz - d, nz) * 2 + 1 - core
         a_in(b, f_send.at[d]).wait_recv()
-
-    def pick(keys, wanted, values, shape):
-        acc = values(0)
-        for i in range(1, nx):
-            acc = jnp.where(jnp.full(shape, keys(i) - wanted) == 0, values(i), acc)
-        return acc
-
-    def deal_of(i):
-        return deal_ref[i]
-
-    def route_of(c):
-        return pick(deal_of, c, lambda i: route_ref[i * new:(i + 1) * new, :], (1, route_ref.shape[1]))
-
-    tile[...] = jnp.zeros_like(tile)
-    gain = gain_ref[...].astype(f32)
-    loads[0].wait()
 
     def scaled_of(c):
         x = pick(deal_of, c, lambda i: xg[i * new:(i + 1) * new, :].astype(f32), (1, xg.shape[1]))
@@ -128,9 +150,9 @@
         q1 = q0
         for e in range(experts):
             y = jnp.dot(xs, wq[e], preferred_element_type=f32)
-            q0 = jnp.where(r0 == e, y, q0)
-            q1 = jnp.where(r1 == e, y, q1)
-        tile[:, 0:experts] = jnp.dot(xs, wr_ref[...], preferred_element_type=f32)
+            q0 = jnp.where(r0 == float(e), y, q0)
+            q1 = jnp.where(r1 == float(e), y, q1)
+        tile[:, 0:experts] = lax.dot_general(xs, wr_ref[...], nt, preferred_element_type=f32)
         tile[:, experts:experts + 1] = jnp.sum(x * x, axis=1, keepdims=True)
         return q0, q1, tile[...].T[0:16]
 
@@ -149,16 +171,14 @@
     qsend[0, 0:new] = q0
     qsend[0, new:rows] = q1
     gsend[0] = g
-    loads[1].wait()
-
     def send_kv(d, carry):
         c = lax.rem(mx + d, nx)
-        kvsend[d] = jnp.dot(scaled_of(c)[1], wkv[...], preferred_element_type=f32)
+        kvsend[d] = jnp.dot(scaled_of(c)[1], wkv[...], preferred_element_type=f32).astype(bf16)
         kv_copy(c, d).start()
         return carry
 
     lax.fori_loop(1, nx, send_kv, 0)
-    kvsend[0] = jnp.dot(scaled_of(mx)[1], wkv[...], preferred_element_type=f32)
+    kvown[...] = jnp.dot(scaled_of(mx)[1], wkv[...], preferred_element_type=f32)
 
     for d in range(1, nx):
         c = lax.rem(mx + d, nx)
@@ -172,7 +192,7 @@
     inv = lax.rsqrt(cols[:, experts:experts + 1] * (1.0 / full_width) + norm_eps)
     inv2 = jnp.concatenate([inv, inv], axis=0)
     route = route_of(mx)
-    lane = lax.broadcasted_iota(jnp.int32, (new, 128), 1)
+    lane = lax.broadcasted_iota(jnp.int32, (new, 128), 1).astype(f32)
     logits = cols * inv
     c0 = jnp.sum(jnp.where(lane == route[:, 0:1], logits, 0.0), axis=1, keepdims=True)
     c1 = jnp.sum(jnp.where(lane == route[:, 1:2], logits, 0.0), axis=1, keepdims=True)
@@ -198,7 +218,6 @@
     bk = min(512, cache)
     length = pick(deal_of, mx, lambda i: jnp.full((1, bk), lengths_ref[i]), (1, bk))
     loads[2].wait()
-    nt = (((1,), (1,)), ((), ()))
     maxes[...] = jnp.full(maxes.shape, masked_score, f32)
 
     def fold_max(h, s):
@@ -223,9 +242,9 @@
     for d in range(1, nx):
         c = lax.rem(mx + d, nx)
         remote(kvsend.at[d], kvrecv.at[c], kv_send.at[d], kv_recv.at[c], atx(c)).wait_recv()
-    kv = kvsend[0]
-    for d in range(1, nx):
-        kv = kv + kvrecv[lax.rem(mx + d, nx)]
+    kv = kvown[...]
+    for d in range(1, nx):
+        kv = kv + kvrecv[lax.rem(mx + d, nx)].astype(f32)
     kv = (kv * inv).astype(bf16)
     row = lax.rem(lax.broadcasted_iota(jnp.int32, (rows, new), 0), new)
     causal = lax.broadcasted_iota(jnp.int32, (rows, new), 1) <= row
@@ -271,10 +290,8 @@
         gate = tile[...].T
         a = [agbuf[c, h] for h in range(heads)]
         a = jnp.concatenate(a, axis=1) if heads > 1 else a[0]
-        y = jnp.zeros((rows, wo.shape[2]), f32)
-        for e in range(experts):
-            y = y + jnp.dot(jnp.where(rr == e, a, jnp.zeros_like(a)), wo[e],
-                            preferred_element_type=f32)
+        spread = [jnp.where(rr == float(e), a, jnp.zeros_like(a)) for e in range(experts)]
+        y = jnp.dot(jnp.concatenate(spread, axis=1), wo[...], preferred_element_type=f32)
         outs[c] = gate[:, 0:1] * y[0:new] + gate[:, 1:2] * y[new:rows]
 
     produce(mx)
@@ -354,17 +371,21 @@
         out_specs=vspec,
         scratch_shapes=[
             vm((total, width), bf16),
+            vm((experts, width, heads, hd), bf16),
+            vm((width, heads, 2 * hd), bf16),
             vm((experts, width, hw), bf16),
             vm((width, 2 * hw), bf16),
-            vm((experts, hw, out_w), bf16),
+            vm((experts * hw, out_w), bf16),
             vm((heads, cache, hd), bf16),
             vm((heads, cache, hd), bf16),
+            vm((nx, new, 128), f32),
             vm((nx, rows, hw), f32),
             vm((nx, rows, hw), f32),
             vm((nx, 16, new), f32),
             vm((nx, 16, new), f32),
-            vm((nx, new, 2 * hw), f32),
-            vm((nx, new, 2 * hw), f32),
+            vm((nx, new, 2 * hw), bf16),
+            vm((nx, new, 2 * hw), bf16),
+            vm((new, 2 * hw), f32),
             vm((new, 128), f32),
             vm((nx, 8, new), f32),
             vm((rows, hw), bf16),
@@ -384,12 +405,12 @@
             dma, dma, dma((nz,)), dma((nz,)),
         ],
         compiler_params=pltpu.CompilerParams(
-            collective_id=0, has_side_effects=True, vmem_limit_bytes=48 * 1024 * 1024
+            collective_id=0, has_side_effects=True, vmem_limit_bytes=60 * 1024 * 1024
         ),
     )(
-        tokens, gain.reshape(1, width), w_router, route, lengths, deal,
-        wq.reshape(experts, width, hw), wkv.reshape(width, 2 * hw),
-        wo.reshape(experts, hw, out_w), ck[0], cv[0],
+        tokens, gain, w_router.T, route.T, lengths, deal,
+        wq, wkv,
+        wo.reshape(experts * hw, out_w), ck[0], cv[0],
     )
 
 

time: 70.9 us -> 58.9 us (0.83)
  local copies, waits for them, and re-layouts: 8.91 us -> 1.47 us
  Pallas kernels: 61.5 us -> 57.3 us
    pallas_call x1, Pallas kernels: 61.5 us -> 57.3 us  [per_device(): pl.pallas_call(functools.partial(kernel, nx, ny, width * nx), out_shape=j...]
    reshape x2 -> x0, local copies, waits for them, and re-layouts: 3.86 us -> none  [the longest x1 3.18 us: per_device(): wq.reshape(experts, width, hw)]
    unnamed x12 -> x1, local copies, waits for them, and re-layouts: 5.05 us -> 1.47 us
where the time goes in v2:
time: 58.9 us; the launch traced here: 58.7 us
  Pallas kernels  57.3 us (97%)
  local copies, waits for them, and re-layouts  1.47 us (2%)
    pallas_call x1, Pallas kernels, per_device(): pl.pallas_call(functools.partial(kernel, nx, ny, width * nx), out_shape=j...  57.3 us
    unnamed x1, local copies, waits for them, and re-layouts  1.47 us

profile of v2, /device:TPU:0, one launch (start us, length us, event | category | flops | bytes accessed | tf_op | source)
XLA Modules:
  0.0 58.7 jit_solution(7110545662536737276)
XLA Ops:
  0.0 57.3 %shard_map.109 = bf16[64,512]{1,0:T(8,128)(2,1)} custom-call(bf16[64,512]{1,0:T(8,128)(2,1)} %tokens_ref.1, bf16[512]{0:T(512)(128)(2,1)} %gain_ref.1, bf16[8,512]{1,0:T(8,128)(2,1)} %bitcast.8, s32[2,512]{1,0:T(2,128)} %bitcast.9, s32[4]{0:T(128)} %lengths_ref.1, s32[4]{0:T(128)} %deal_ref.1, bf16[8,512,2,128]{3,2,1,0:T(2,128)(2,1)} %wq_hbm.1, ...), custom_call_target="tpu_custom_call" | custom-call | tf_op jit(solution)/shard_map/pallas_call | solution.py:367
  57.3 1.5 %copy.13 = bf16[64,512]{1,0:T(8,128)(2,1)} copy(bf16[64,512]{1,0:T(8,128)(2,1)} %shard_map.109) | data formatting | bytes 131072

commit v3 on v2

--- a/solution.py
+++ b/solution.py
@@ -311,11 +311,13 @@
         part = pl.ds(pl.multiple_of(lax.rem(b, per_req) * tb, tb), tb)
         return pick(lambda i: i, slot, lambda i: outs[i, part, :], (1, outs.shape[2]))
 
-    for z in range(nz):
-        psend[z] = partial(z * 2 + 1 - core)
-    pc = remote(psend, precv, p_send, p_recv, aty(partner))
-    pc.start()
-    pc.wait_recv()
+    def p_copy(z):
+        return remote(psend.at[z], precv.at[z], p_send.at[z], p_recv.at[z], aty(partner))
+
+    for d in range(nz - 1, -1, -1):
+        z = lax.rem(mz + d, nz)
+        psend[z] = partial(z * 2 + 1 - core).astype(bf16)
+        p_copy(z).start()
 
     def z_copy(d, at):
         return remote(zsend.at[d], zrecv.at[at], z_send.at[d], z_recv.at[at],
@@ -323,9 +325,11 @@
 
     for d in range(nz - 1, 0, -1):
         z = lax.rem(mz + d, nz)
-        zsend[d] = (partial(z * 2 + core) + precv[z]).astype(bf16)
+        p_copy(z).wait_recv()
+        zsend[d] = (partial(z * 2 + core) + precv[z].astype(f32)).astype(bf16)
         z_copy(d, mz).start()
-    total = partial(my) + precv[mz]
+    p_copy(mz).wait_recv()
+    total = partial(my) + precv[mz].astype(f32)
     for d in range(1, nz):
         z = lax.rem(mz + nz - d, nz)
         z_copy(d, z).wait_recv()
@@ -337,7 +341,8 @@
         a_copy(d).wait_send()
         a_in(lax.rem(mz + nz - d, nz) * 2 + core, f_send.at[d]).wait_send()
         z_copy(d, mz).wait_send()
-    pc.wait_send()
+    for z in range(nz):
+        p_copy(z).wait_send()
     for d in range(1, nx):
         c = lax.rem(mx + d, nx)
         g_copy(c, d).wait_send()
@@ -395,14 +400,14 @@
             vm((new, hd), bf16),
             vm((nx, heads, rows, hd), bf16),
             vm((nx, new, out_w), f32),
-            vm((nz, tb, out_w), f32),
-            vm((nz, tb, out_w), f32),
+            vm((nz, tb, out_w), bf16),
+            vm((nz, tb, out_w), bf16),
             vm((nz, tb, out_w), bf16),
             vm((nz, tb, out_w), bf16),
             dma((5,)), dma((nz,)), dma((ny,)), dma((nz,)),
             dma((nx,)), dma((nx,)), dma((nx,)), dma((nx,)), dma((nx,)), dma((nx,)),
             dma((nx,)), dma((nx,)), dma((heads, nx)), dma((heads, nx)),
-            dma, dma, dma((nz,)), dma((nz,)),
+            dma((nz,)), dma((nz,)), dma((nz,)), dma((nz,)),
         ],
         compiler_params=pltpu.CompilerParams(
             collective_id=0, has_side_effects=True, vmem_limit_bytes=60 * 1024 * 1024

time: 58.9 us -> 58.3 us (0.990)
  Pallas kernels: 57.3 us -> 56.6 us
    pallas_call x1, Pallas kernels: 57.3 us -> 56.6 us  [per_device(): pl.pallas_call(functools.partial(kernel, nx, ny, width * nx), out_shape=j...]
where the time goes in v3:
time: 58.3 us; the launch traced here: 58.1 us
  Pallas kernels  56.6 us (97%)
  local copies, waits for them, and re-layouts  1.47 us (3%)
    pallas_call x1, Pallas kernels, per_device(): pl.pallas_call(functools.partial(kernel, nx, ny, width * nx), out_shape=j...  56.6 us
    unnamed x1, local copies, waits for them, and re-layouts  1.47 us

profile of v3, /device:TPU:0, one launch (start us, length us, event | category | flops | bytes accessed | tf_op | source)
XLA Modules:
  0.0 58.1 jit_solution(11912370324885839261)
XLA Ops:
  0.0 56.6 %shard_map.109 = bf16[64,512]{1,0:T(8,128)(2,1)} custom-call(bf16[64,512]{1,0:T(8,128)(2,1)} %tokens_ref.1, bf16[512]{0:T(512)(128)(2,1)} %gain_ref.1, bf16[8,512]{1,0:T(8,128)(2,1)} %bitcast.8, s32[2,512]{1,0:T(2,128)} %bitcast.9, s32[4]{0:T(128)} %lengths_ref.1, s32[4]{0:T(128)} %deal_ref.1, bf16[8,512,2,128]{3,2,1,0:T(2,128)(2,1)} %wq_hbm.1, ...), custom_call_target="tpu_custom_call" | custom-call | tf_op jit(solution)/shard_map/pallas_call | solution.py:372
  56.6 1.5 %copy.13 = bf16[64,512]{1,0:T(8,128)(2,1)} copy(bf16[64,512]{1,0:T(8,128)(2,1)} %shard_map.109) | data formatting | bytes 131072

commit v4 on v3

--- a/solution.py
+++ b/solution.py
@@ -114,10 +114,6 @@
         return carry
 
     lax.fori_loop(0, experts, relayout, 0)
-    loads[1].wait()
-    for h in range(heads):
-        wkv[:, h * 2 * hd:(h + 1) * 2 * hd] = wkv3[:, h, :]
-
 
     for d in range(1, nz):
         b = lax.rem(mz + nz - d, nz) * 2 + core
@@ -171,6 +167,10 @@
     qsend[0, 0:new] = q0
     qsend[0, new:rows] = q1
     gsend[0] = g
+    loads[1].wait()
+    for h in range(heads):
+        wkv[:, h * 2 * hd:(h + 1) * 2 * hd] = wkv3[:, h, :]
+
     def send_kv(d, carry):
         c = lax.rem(mx + d, nx)
         kvsend[d] = jnp.dot(scaled_of(c)[1], wkv[...], preferred_element_type=f32).astype(bf16)

time: 58.3 us -> 57.5 us (0.986)
  Pallas kernels: 56.6 us -> 55.9 us
    pallas_call x1, Pallas kernels: 56.6 us -> 55.9 us  [per_device(): pl.pallas_call(functools.partial(kernel, nx, ny, width * nx), out_shape=j...]
where the time goes in v4:
time: 57.5 us; the launch traced here: 57.3 us
  Pallas kernels  55.9 us (97%)
  local copies, waits for them, and re-layouts  1.47 us (3%)
    pallas_call x1, Pallas kernels, per_device(): pl.pallas_call(functools.partial(kernel, nx, ny, width * nx), out_shape=j...  55.9 us
    unnamed x1, local copies, waits for them, and re-layouts  1.47 us

profile of v4, /device:TPU:0, one launch (start us, length us, event | category | flops | bytes accessed | tf_op | source)
XLA Modules:
  0.0 57.3 jit_solution(9496194854364614689)
XLA Ops:
  0.0 55.9 %shard_map.109 = bf16[64,512]{1,0:T(8,128)(2,1)} custom-call(bf16[64,512]{1,0:T(8,128)(2,1)} %tokens_ref.1, bf16[512]{0:T(512)(128)(2,1)} %gain_ref.1, bf16[8,512]{1,0:T(8,128)(2,1)} %bitcast.8, s32[2,512]{1,0:T(2,128)} %bitcast.9, s32[4]{0:T(128)} %lengths_ref.1, s32[4]{0:T(128)} %deal_ref.1, bf16[8,512,2,128]{3,2,1,0:T(2,128)(2,1)} %wq_hbm.1, ...), custom_call_target="tpu_custom_call" | custom-call | tf_op jit(solution)/shard_map/pallas_call | solution.py:372
  55.9 1.5 %copy.13 = bf16[64,512]{1,0:T(8,128)(2,1)} copy(bf16[64,512]{1,0:T(8,128)(2,1)} %shard_map.109) | data formatting | bytes 131072
